TPU v7x, 128 devices: a whole 4x4x4 slice. The times are simulated.
128 devices in a mesh: gx: 16 (over x_hi, y, core), gy: 8 (over x_lo, z).
Axes of the slice: x: 4 (x_hi: 2, x_lo: 2; x = x_hi * 2 + x_lo), y: 4, z: 4, core: 2. Of those that a mesh axis runs over, the one named last changes fastest.
Arguments:
- flow_field: bfloat16 [4, 64, 1024, 512], P(None, None, ('gx', 'gy')), may hold values from -6 to 6
- cotangent: bfloat16 [4, 64, 1024, 512], P(None, None, ('gx', 'gy')), may hold values from -2 to 2
- spectral_weight: bfloat16 [128, 64, 64, 128], P(('gx', 'gy')), may hold values from -0.75 to 0.75
- local_weight: bfloat16 [64, 64], replicated, may hold values from -0.75 to 0.75
- channel_bias: float32 [64], replicated, may hold values from -3 to 3
Outputs:
- output_field: bfloat16 [4, 64, 1024, 512], P(None, None, ('gx', 'gy'))
- grad_field: bfloat16 [4, 64, 1024, 512], P(None, None, ('gx', 'gy'))
- grad_spectral: float32 [128, 64, 64, 128], P(('gx', 'gy'))
All inputs are finite; a program needn't handle non-finite values.
Results may differ from a plain program's by a relative error of at most 0.014.
Values may be sent and summed in bfloat16 or wider, within the bound.
No kernel may reach another device: no remote copies, remote signals or barrier semaphores. Data moves between devices by JAX's collectives and lax.ppermute only.
A program may use at most 64 MiB of HBM per device.

v0:
```python
import functools
import math

import jax
import jax.numpy as jnp
import numpy as np
from jax import lax
from jax.experimental import pallas as pl
from jax.experimental.pallas import tpu as pltpu
from jax.sharding import PartitionSpec as P

AXES = ("gx", "gy")
LANES = 128
VMEM_LIMIT = 20 * 1024 * 1024

ROOT_HALF = 0.7071067811865476
HALF_LOG2E = 0.5 * math.log2(math.e)
DENSITY = 0.3989422804014327


def basis_table(cells, kept, factor):
    positions = np.arange(cells, dtype=np.int64)
    columns = np.arange(2 * kept, dtype=np.int64)
    frequency = np.where(columns < kept, columns, columns - kept + 1)
    phases = positions[:, None] * frequency[None, :] % cells
    angles = phases.astype(np.float32) * np.float32(2.0 * math.pi / cells)
    values = np.where(columns[None, :] < kept, np.cos(angles), np.sin(angles))
    return (values * np.float32(factor)).astype(jnp.bfloat16)


def dot(a, b, contract):
    return lax.dot_general(a, b, (contract, ((), ())), preferred_element_type=jnp.float32)


def in_hbm(array):
    return pltpu.with_memory_space_constraint(array, pltpu.MemorySpace.HBM)


def params():
    return pltpu.CompilerParams(vmem_limit_bytes=VMEM_LIMIT)


def rows_to_blocks(half, slab, by_rows, by_peer):
    tiles = 2 * slab
    for x in range(slab):
        part = by_rows[pl.ds(half * LANES * slab + x, LANES, stride=slab), :]
        by_peer[pl.ds(half * slab + x, LANES, stride=tiles), :] = part.T


def blocks_to_rows(blocks_ref, slab, by_peer, by_rows):
    tiles = 2 * slab
    by_peer[...] = blocks_ref[...].astype(jnp.float32)
    for half in range(2):
        for x in range(slab):
            part = by_peer[pl.ds(half * slab + x, LANES, stride=tiles), :]
            by_rows[pl.ds(half * LANES * slab + x, LANES, stride=slab), :] = part.T


def fetch(pairs, sems):
    copies = [pltpu.make_async_copy(source, target, sems.at[i]) for i, (source, target) in enumerate(pairs)]
    for copy in copies:
        copy.start()
    return copies


def part_of(ref, index, parts):
    rows = ref.shape[0] // parts
    return ref.at[pl.ds(pl.multiple_of(index * rows, rows), rows), :]


def analysis_kernel(slab, pieces, field_hbm, table_hbm, out_ref, by_rows, by_peer, field, table, sems):
    pairs = [(table_hbm, table)]
    pairs += [(part_of(field_hbm, i, 2 * pieces), part_of(field, i, 2 * pieces)) for i in range(pieces)]
    pairs += [(part_of(field_hbm, 1, 2), part_of(field, 1, 2))]
    copies = fetch(pairs, sems)
    for half in range(2):
        for copy in copies[-1:] if half else copies[:-1]:
            copy.wait()
        part_of(by_rows, half, 2)[...] = dot(part_of(field, half, 2)[...], table[...], ((1,), (0,)))
        rows_to_blocks(half, slab, by_rows, by_peer)
    out_ref[...] = by_peer[...].astype(out_ref.dtype)


EVERY = pl.BlockSpec(memory_space=pltpu.VMEM)
ANYWHERE = pl.BlockSpec(memory_space=pl.ANY)


def analysis(field, table):
    total, cells = field.shape
    peers = table.shape[1]
    slab = total // (2 * LANES)
    pieces = 4
    return pl.pallas_call(
        functools.partial(analysis_kernel, slab, pieces),
        out_shape=jax.ShapeDtypeStruct((peers * 2 * slab, LANES), jnp.bfloat16),
        in_specs=[ANYWHERE, ANYWHERE],
        out_specs=EVERY,
        scratch_shapes=[
            pltpu.VMEM((total, peers), jnp.float32),
            pltpu.VMEM((peers * 2 * slab, LANES), jnp.float32),
            pltpu.VMEM(field.shape, field.dtype),
            pltpu.VMEM(table.shape, table.dtype),
            pltpu.SemaphoreType.DMA((2 + pieces,)),
        ],
        compiler_params=params(),
        cost_estimate=pl.CostEstimate(flops=2 * total * cells * peers, bytes_accessed=3 << 20, transcendentals=0),
        name="analysis",
    )(in_hbm(field), in_hbm(table))


def mixing_matrix(spread_ref, weight_ref, slab, axis):
    spread = spread_ref[...]
    wide = dot(spread, weight_ref[...], ((1,), (axis,))).astype(jnp.bfloat16)
    full = dot(wide, spread, ((1,), (1,)))
    row = lax.broadcasted_iota(jnp.int32, full.shape, 0) % slab
    col = lax.broadcasted_iota(jnp.int32, full.shape, 1) % slab
    return jnp.where(row == col, full, 0.0).astype(jnp.bfloat16)


def owner_kernel(forward, slab, blocks_ref, into_ref, back_ref, weight_ref, out_ref, modes_ref, kept, mixed, partial, out, sems):
    peers = blocks_ref.shape[0] // (2 * slab)
    channels = weight_ref.shape[0]
    planes = 2 * LANES // channels
    received = blocks_ref[...].astype(jnp.float32).reshape(peers, 2 * slab, LANES)
    for half in range(2):
        part = received[:, half * slab : (half + 1) * slab, :].reshape(peers * slab, LANES).astype(jnp.bfloat16)
        modes = dot(into_ref[...], part, ((1,), (0,))).T
        kept[half * LANES : (half + 1) * LANES, :] = modes.astype(jnp.bfloat16).astype(jnp.float32)
    modes_ref[...] = kept[...].astype(jnp.bfloat16)
    if forward:

        def step(i, sums):
            weight = weight_ref[i].astype(jnp.float32)
            return tuple(sums[z] + kept[pl.ds(z * channels + i, 1), :] * weight for z in range(planes))

        zeros = jnp.zeros((channels, LANES), jnp.float32)
        sums = lax.fori_loop(0, channels, step, (zeros,) * planes, unroll=16)
        for z in range(planes):
            mixed[z * channels : (z + 1) * channels, :] = sums[z]
    else:

        def step(i, carry):
            weight = weight_ref[i].astype(jnp.float32)
            for z in range(planes):
                product = weight * kept[z * channels : (z + 1) * channels, :]
                folded = product.reshape(channels // 8, 8, LANES).sum(axis=0)
                partial[pl.ds((z * channels + i) * 8, 8), :] = folded
            return carry

        for i in range(channels):
            step(i, 0)
        total = partial[pl.ds(0, planes * channels, stride=8), :]
        for row in range(1, 8):
            total = total + partial[pl.ds(row, planes * channels, stride=8), :]
        mixed[...] = total
    pieces = 1 if forward else 4
    group = peers // pieces
    sent = []
    for i in range(pieces):
        halves = []
        for half in range(2):
            part = mixed[half * LANES : (half + 1) * LANES, :].astype(jnp.bfloat16)
            spatial = dot(back_ref[i * group * slab : (i + 1) * group * slab, :], part, ((1,), (1,)))
            halves.append(spatial.reshape(group, slab, LANES))
        tiles = jnp.concatenate(halves, axis=1).reshape(group * 2 * slab, LANES).astype(out_ref.dtype)
        if forward:
            out_ref[...] = tiles
        else:
            part_of(out, i, pieces)[...] = tiles
            sent.append(pltpu.make_async_copy(part_of(out, i, pieces), part_of(out_ref, i, pieces), sems.at[i]))
            sent[i].start()
    for copy in sent:
        copy.wait()


def owner(blocks, into, back, weight, forward):
    cells, modes = back.shape
    rows = blocks.shape[0]
    channels = weight.shape[0]
    slab = rows // (2 * LANES)
    return pl.pallas_call(
        functools.partial(owner_kernel, forward, slab),
        out_shape=(
            (jax.ShapeDtypeStruct if forward else pltpu.MemorySpace.HBM)(blocks.shape, jnp.bfloat16),
            jax.ShapeDtypeStruct((2 * LANES, modes), jnp.bfloat16),
        ),
        in_specs=[EVERY] * 4,
        out_specs=(EVERY if forward else ANYWHERE, EVERY),
        scratch_shapes=[
            pltpu.VMEM((2 * LANES, modes), jnp.float32),
            pltpu.VMEM((2 * LANES, modes), jnp.float32),
            pltpu.VMEM((8 if forward else 8 * 2 * LANES, modes), jnp.float32),
            pltpu.VMEM((16, LANES) if forward else blocks.shape, jnp.bfloat16),
            pltpu.SemaphoreType.DMA((4,)),
        ],
        compiler_params=params(),
        cost_estimate=pl.CostEstimate(flops=4 * rows * LANES * modes, bytes_accessed=4 << 20, transcendentals=0),
        name="owner_forward" if forward else "owner_backward",
    )(blocks, into, back, weight)


def slab_kernel(slab, planes, chunk, blocks_ref, field_ref, weight_ref, spread_ref, bias_ref, cotangent_ref, synth_ref,
                table_ref, out_hbm, grad_ref, send_ref, by_peer, by_rows, half_rows, pre_even, pre_odd, matrix, offset, out,
                out_sems):
    plane_rows = out.shape[0] // planes
    rows = plane_rows // 2

    def out_copy(i):
        return pltpu.make_async_copy(part_of(out, i, 2 * planes), part_of(out_hbm, i, 2 * planes), out_sems.at[i])

    def fill(target, z, half):
        start = z * plane_rows + half * rows
        modal = by_rows[pl.ds(start, rows), :].astype(jnp.bfloat16)
        mix = matrix[half * rows : (half + 1) * rows, :]
        local = dot(mix, part_of(field_ref, z, planes)[...], ((1,), (0,)))
        target[...] = dot(modal, synth_ref[...], ((1,), (0,))) + local + offset[half * rows : (half + 1) * rows, :]

    def activate(source, z, half):
        start = z * plane_rows + half * rows
        for index in range(rows // chunk):
            there = pl.ds(start + index * chunk, chunk)
            value = source[index * chunk : (index + 1) * chunk, :]
            share = 0.5 + 0.5 * lax.erf(value * ROOT_HALF)
            bell = jnp.exp2(value * value * -HALF_LOG2E)
            out[there, :] = (value * share).astype(out.dtype)
            slope = share + value * bell * DENSITY
            grad_ref[there, :] = (cotangent_ref[there, :].astype(jnp.float32) * slope).astype(grad_ref.dtype)
        out_copy(2 * z + half).start()

    def analyse(z, half):
        here = pl.ds(z * plane_rows + half * rows, rows)
        half_rows[here, :] = dot(grad_ref[here, :], table_ref[...], ((1,), (0,)))

    matrix[...] = mixing_matrix(spread_ref, weight_ref, slab, 1)
    offset[...] = jnp.sum(spread_ref[...].astype(jnp.float32) * bias_ref[...], axis=1, keepdims=True)
    blocks_to_rows(blocks_ref, slab, by_peer, by_rows)
    fill(pre_even, 0, 0)

    def plane(z):
        fill(pre_odd, z, 1)
        activate(pre_even, z, 0)
        analyse(z, 0)
        if z + 1 < planes:
            fill(pre_even, z + 1, 0)
        activate(pre_odd, z, 1)
        analyse(z, 1)

    for z in range(planes):
        plane(z)
    for half in range(2):
        rows_to_blocks(half, slab, half_rows, by_peer)
    send_ref[...] = by_peer[...].astype(send_ref.dtype)
    for i in range(2 * planes):
        out_copy(i).wait()


def spread_table(channels, slab):
    return jnp.asarray(np.kron(np.eye(channels), np.ones((slab, 1))).astype(jnp.bfloat16))


def slab_stage(blocks, field, cotangent, weight, bias, synth, table):
    total, cells = cotangent.shape
    modes = table.shape[1]
    slab = total // (2 * LANES)
    channels = weight.shape[0]
    planes = 2 * LANES // channels
    rows = total // planes
    whole = (total, cells)
    return pl.pallas_call(
        functools.partial(slab_kernel, slab, planes, 16),
        out_shape=(
            pltpu.MemorySpace.HBM(whole, jnp.bfloat16),
            jax.ShapeDtypeStruct(whole, jnp.bfloat16),
            jax.ShapeDtypeStruct(blocks.shape, jnp.bfloat16),
        ),
        in_specs=[EVERY] * 8,
        out_specs=(ANYWHERE, EVERY, EVERY),
        scratch_shapes=[
            pltpu.VMEM((total, modes), jnp.float32),
            pltpu.VMEM((total, modes), jnp.float32),
            pltpu.VMEM((total, modes), jnp.float32),
            pltpu.VMEM((rows // 2, cells), jnp.float32),
            pltpu.VMEM((rows // 2, cells), jnp.float32),
            pltpu.VMEM((rows, rows), jnp.bfloat16),
            pltpu.VMEM((rows, 1), jnp.float32),
            pltpu.VMEM(whole, jnp.bfloat16),
            pltpu.SemaphoreType.DMA((2 * planes,)),
        ],
        compiler_params=params(),
        cost_estimate=pl.CostEstimate(flops=4 * total * cells * modes, bytes_accessed=11 << 20, transcendentals=2 * total * cells),
        name="slab_stage",
    )(blocks, field, weight, spread_table(channels, slab), bias, cotangent, synth, table)


def pointwise_kernel(slab, planes, field_ref, weight_ref, spread_ref, out_ref, matrix, result, sem):
    matrix[...] = mixing_matrix(spread_ref, weight_ref, slab, 0)
    for z in range(planes):
        product = dot(matrix[...], part_of(field_ref, z, planes)[...], ((1,), (0,)))
        part_of(result, z, planes)[...] = product.astype(result.dtype)
    copy = pltpu.make_async_copy(result, out_ref, sem)
    copy.start()
    copy.wait()


def pointwise(field, weight):
    total, cells = field.shape
    channels = weight.shape[0]
    planes = 2 * LANES // channels
    rows = total // planes
    slab = rows // channels
    return pl.pallas_call(
        functools.partial(pointwise_kernel, slab, planes),
        out_shape=jax.ShapeDtypeStruct((total, cells), jnp.bfloat16),
        in_specs=[EVERY] * 3,
        out_specs=EVERY,
        scratch_shapes=[
            pltpu.VMEM((rows, rows), jnp.bfloat16),
            pltpu.VMEM((total, cells), jnp.bfloat16),
            pltpu.SemaphoreType.DMA,
        ],
        input_output_aliases={0: 0},
        compiler_params=params(),
        cost_estimate=pl.CostEstimate(flops=2 * total * rows * cells, bytes_accessed=6 << 20, transcendentals=0),
        name="pointwise",
    )(field, weight, spread_table(channels, slab))


def final_kernel(slab, planes, blocks_ref, through_ref, synth_ref, out_hbm, by_peer, by_rows, out, out_sems):
    blocks_to_rows(blocks_ref, slab, by_peer, by_rows)
    sends = [pltpu.make_async_copy(part_of(out, z, planes), part_of(out_hbm, z, planes), out_sems.at[z]) for z in range(planes)]
    for z in range(planes):
        modal = part_of(by_rows, z, planes)[...].astype(jnp.bfloat16)
        through = part_of(through_ref, z, planes)[...].astype(jnp.float32)
        part_of(out, z, planes)[...] = (dot(modal, synth_ref[...], ((1,), (0,))) + through).astype(out.dtype)
        sends[z].start()
    for send in sends:
        send.wait()


def final_stage(blocks, through, synth):
    total, cells = through.shape
    modes = synth.shape[0]
    slab = total // (2 * LANES)
    planes = 4
    return pl.pallas_call(
        functools.partial(final_kernel, slab, planes),
        out_shape=pltpu.MemorySpace.HBM((total, cells), jnp.bfloat16),
        in_specs=[EVERY] * 3,
        out_specs=ANYWHERE,
        scratch_shapes=[
            pltpu.VMEM((total, modes), jnp.float32),
            pltpu.VMEM((total, modes), jnp.float32),
            pltpu.VMEM((total, cells), jnp.bfloat16),
            pltpu.SemaphoreType.DMA((planes,)),
        ],
        compiler_params=params(),
        cost_estimate=pl.CostEstimate(flops=2 * total * cells * modes, bytes_accessed=7 << 20, transcendentals=0),
        name="final_stage",
    )(blocks, through, synth)


def weight_grad_kernel(step_channels, coeffs_ref, grads_ref, out_ref):
    channels = out_ref.shape[1]
    planes = coeffs_ref.shape[0] // channels
    first = pl.program_id(0) * step_channels

    def step(i, carry):
        total = None
        for z in range(planes):
            row = coeffs_ref[pl.ds(z * channels + first + i, 1), :]
            term = row * grads_ref[z * channels : (z + 1) * channels, :]
            total = term if total is None else total + term
        out_ref[i] = total
        return carry

    lax.fori_loop(0, step_channels, step, 0, unroll=4)


def weight_grad(coeffs, grads, channels):
    modes = coeffs.shape[1]
    step_channels = 16
    fixed = pl.BlockSpec(coeffs.shape, lambda s: (0, 0))
    return pl.pallas_call(
        functools.partial(weight_grad_kernel, step_channels),
        out_shape=jax.ShapeDtypeStruct((channels, channels, modes), jnp.float32),
        grid=(channels // step_channels,),
        in_specs=[fixed, fixed],
        out_specs=pl.BlockSpec((step_channels, channels, modes), lambda s: (s, 0, 0)),
        compiler_params=params(),
        cost_estimate=pl.CostEstimate(flops=2 * coeffs.size * channels, bytes_accessed=5 << 20, transcendentals=0),
        name="weight_grad",
    )(coeffs, grads)


def exchange(blocks, devices):
    tiles = blocks.reshape(devices, blocks.shape[0] // devices, LANES)
    return lax.all_to_all(tiles, AXES, split_axis=0, concat_axis=0, tiled=True).reshape(blocks.shape)


def shards(flow_field, cotangent, spectral_weight, local_weight, channel_bias):
    devices = lax.axis_size("gx") * lax.axis_size("gy")
    planes, channels, slab, cells_along = flow_field.shape
    cells_across = slab * devices
    kept = spectral_weight.shape[3] // 2
    forward_x = basis_table(cells_across, kept, math.sqrt(2.0 / cells_across))
    forward_y = basis_table(cells_along, kept, math.sqrt(2.0 / cells_along))
    inverse_x = basis_table(cells_across, kept, math.sqrt(1.0 / kept))
    inverse_y = basis_table(cells_along, kept, math.sqrt(1.0 / kept))

    def flip(table):
        return jnp.asarray(np.ascontiguousarray(table.T))

    field = flow_field.reshape(planes * channels * slab, cells_along)
    gradient = cotangent.reshape(field.shape)
    weight = spectral_weight.reshape(spectral_weight.shape[1:])
    bias = channel_bias[None, :]

    received = exchange(analysis(field, jnp.asarray(forward_y)), devices)
    modal, coeffs = owner(received, flip(forward_x), jnp.asarray(inverse_x), weight, True)
    gathered = exchange(modal, devices)
    output, grad_pre, grad_rows = slab_stage(
        gathered, field, gradient, local_weight, bias, flip(inverse_y), jnp.asarray(inverse_y)
    )
    received = exchange(grad_rows, devices)
    partial, grads = owner(received, flip(inverse_x), jnp.asarray(forward_x), weight, False)
    gathered = exchange(partial, devices)
    grad_weight = weight_grad(coeffs.astype(jnp.float32), grads.astype(jnp.float32), channels)
    grad_field = final_stage(gathered, pointwise(grad_pre, local_weight), flip(forward_y))
    return (
        output.reshape(flow_field.shape),
        grad_field.reshape(flow_field.shape),
        grad_weight.reshape(spectral_weight.shape),
    )


def solution(mesh):
    placed = (
        P(None, None, AXES, None),
        P(None, None, AXES, None),
        P(AXES, None, None, None),
        P(),
        P(),
    )
    return jax.shard_map(
        shards,
        mesh=mesh,
        in_specs=placed,
        out_specs=(P(None, None, AXES, None), P(None, None, AXES, None), P(AXES, None, None, None)),
        check_vma=False,
    )
```

profile of v0, /device:TPU:1, one launch (start us, length us, event | category | flops | bytes accessed | tf_op | source)
XLA Modules:
  0.0 93.1 jit_solution(2947216573683055805)
XLA Ops:
  0.6 0.0 copy-start.6
  0.6 0.0 copy-start.7
  0.7 0.0 copy-start.3
  0.7 0.0 copy-start.9
  0.7 0.0 copy-start.10
  0.7 3.3 %analysis.1 = bf16[2048,128]{1,0:T(8,128)(2,1)S(1)} custom-call(bf16[2048,512]{1,0:T(8,128)(2,1)} %bitcast.15, bf16[512,128]{1,0:T(8,128)(2,1)} %constant.18.clone.table_hbm), custom_call_target="tpu_custom_call" | custom-call | flops 268435456 | bytes 3145728 | tf_op jit(solution)/shard_map/analysis/pallas_call | solution.py:93
  4.0 0.0 copy-start
  4.1 0.0 copy-start.2
  4.1 0.0 copy-start.12
  4.1 24.9 %all_to_all.20 = bf16[128,16,128]{2,1,0:T(8,128)(2,1)S(1)} all-to-all(bf16[128,16,128]{2,1,0:T(8,128)(2,1)S(1)} %bitcast.22), channel_id=1, replica_groups=mesh['gx'=16,'gy'=8] {'gx','gy'}, dimensions={0} | all-to-all | bytes 1048576 | tf_op jit(solution)/shard_map/all_to_all | solution.py:397
  28.9 0.0 copy-done.1
  29.0 1.3 %owner_forward.1 = (bf16[2048,128]{1,0:T(8,128)(2,1)S(1)}, bf16[256,128]{1,0:T(8,128)(2,1)S(1)}) custom-call(bf16[2048,128]{1,0:T(8,128)(2,1)S(1)} %bitcast.20, bf16[128,1024]{1,0:T(8,128)(2,1)S(1)} %copy-done.6, bf16[1024,128]{1,0:T(8,128)(2,1)S(1)} %copy-done.7, bf16[64,64,128]{2,1,0:T(8,128)(2,1)S(1)} %bitcast.17), custom_call_target="tpu_custom_call" | custom-call | flops 134217728 | bytes 4194304 | tf_op jit(solution)/shard_map/owner_forward/pallas_call | solution.py:181
  30.3 17.7 %all_to_all.21 = bf16[128,16,128]{2,1,0:T(8,128)(2,1)S(1)} all-to-all(bf16[128,16,128]{2,1,0:T(8,128)(2,1)S(1)} %bitcast.26), channel_id=1, replica_groups=mesh['gx'=16,'gy'=8] {'gx','gy'}, dimensions={0} | all-to-all | bytes 1048576 | tf_op jit(solution)/shard_map/all_to_all | solution.py:397
  48.0 0.0 copy-start.4
  48.0 0.0 copy-start.5
  48.0 5.1 %slab_stage.1 = (bf16[2048,512]{1,0:T(8,128)(2,1)}, bf16[2048,512]{1,0:T(8,128)(2,1)S(1)}, bf16[2048,128]{1,0:T(8,128)(2,1)S(1)}) custom-call(bf16[2048,128]{1,0:T(8,128)(2,1)S(1)} %bitcast.24, bf16[2048,512]{1,0:T(8,128)(2,1)S(1)} %bitcast.16, bf16[64,64]{1,0:T(8,128)(2,1)S(1)} %copy-done.11, bf16[512,64]{1,0:T(8,128)(2,1)S(1)} %copy-done.3, ...), custom_call_target="tpu_custom_call" | custom-call | flops 536870912 | bytes 11534336 | tf_op jit(solution)/shard_map/slab_stage/pallas_call | solution.py:269
  53.1 17.7 %all_to_all.22 = bf16[128,16,128]{2,1,0:T(8,128)(2,1)S(1)} all-to-all(bf16[128,16,128]{2,1,0:T(8,128)(2,1)S(1)} %bitcast.25), channel_id=1, replica_groups=mesh['gx'=16,'gy'=8] {'gx','gy'}, dimensions={0} | all-to-all | bytes 1048576 | tf_op jit(solution)/shard_map/all_to_all | solution.py:397
  70.8 2.0 %owner_backward.1 = (bf16[2048,128]{1,0:T(8,128)(2,1)}, bf16[256,128]{1,0:T(8,128)(2,1)S(1)}) custom-call(bf16[2048,128]{1,0:T(8,128)(2,1)S(1)} %bitcast.21, bf16[128,1024]{1,0:T(8,128)(2,1)S(1)} %copy-done.4, bf16[1024,128]{1,0:T(8,128)(2,1)S(1)} %copy-done.5, bf16[64,64,128]{2,1,0:T(8,128)(2,1)S(1)} %bitcast.18), custom_call_target="tpu_custom_call" | custom-call | flops 134217728 | bytes 4194304 | tf_op jit(solution)/shard_map/owner_backward/pallas_call | solution.py:181
  72.8 4.6 %all-to-all-start.3 = ((bf16[128,16,128]{2,1,0:T(8,128)(2,1)}), bf16[128,16,128]{2,1,0:T(8,128)(2,1)S(1)}, u32[]{:S(2)}, u32[]{:S(2)}) async-start(bf16[128,16,128]{2,1,0:T(8,128)(2,1)} %bitcast.30), calls=%async_computation.3 | async-start | bytes 1048576 | tf_op jit(solution)/shard_map/all_to_all | solution.py:397
  77.4 1.7 %pointwise.1.through_ref = bf16[2048,512]{1,0:T(8,128)(2,1)S(1)} custom-call(bf16[2048,512]{1,0:T(8,128)(2,1)S(1)} %get-tuple-element.14.field_ref, bf16[64,64]{1,0:T(8,128)(2,1)S(1)} %copy-done.11, bf16[512,64]{1,0:T(8,128)(2,1)S(1)} %copy-done.3), custom_call_target="tpu_custom_call", output_to_operand_aliasing={{}: (0, {})} | custom-call | flops 1073741824 | bytes 6291456 | tf_op jit(solution)/shard_map/pointwise/pallas_call | solution.py:311
  79.1 0.0 copy-start.8
  79.1 2.1 %weight_grad.1 = f32[64,64,128]{2,1,0:T(8,128)} custom-call(f32[256,128]{1,0:T(8,128)S(1)} %convert_element_type.6.coeffs_ref, f32[256,128]{1,0:T(8,128)S(1)} %convert_element_type.7.grads_ref), custom_call_target="tpu_custom_call" | custom-call | flops 4194304 | bytes 5242880 | tf_op jit(solution)/shard_map/weight_grad/pallas_call | solution.py:383
  81.2 9.9 %all-to-all-done.3 = bf16[128,16,128]{2,1,0:T(8,128)(2,1)S(1)} async-done(((bf16[128,16,128]{2,1,0:T(8,128)(2,1)}), bf16[128,16,128]{2,1,0:T(8,128)(2,1)S(1)}, u32[]{:S(2)}, u32[]{:S(2)}) %all-to-all-start.3) | async-done | bytes 524320 | tf_op jit(solution)/shard_map/all_to_all | solution.py:397
  91.1 2.0 %final_stage.1 = bf16[2048,512]{1,0:T(8,128)(2,1)} custom-call(bf16[2048,128]{1,0:T(8,128)(2,1)S(1)} %bitcast.19, bf16[2048,512]{1,0:T(8,128)(2,1)S(1)} %pointwise.1.through_ref, bf16[128,512]{1,0:T(8,128)(2,1)S(1)} %copy-done.8), custom_call_target="tpu_custom_call" | custom-call | flops 268435456 | bytes 7340032 | tf_op jit(solution)/shard_map/final_stage/pallas_call | solution.py:345
  (16 shorter events, 0.1 us)
Async XLA Ops:
  0.6 28.3 %copy-start.6 = (bf16[128,1024]{1,0:T(8,128)(2,1)S(1)}, bf16[128,1024]{1,0:T(8,128)(2,1)}, u32[]{:S(2)}) copy-start(bf16[128,1024]{1,0:T(8,128)(2,1)} %constant.19.clone.into_ref) | copy-start | bytes 786436
  0.6 28.3 %copy-start.7 = (bf16[1024,128]{1,0:T(8,128)(2,1)S(1)}, bf16[1024,128]{1,0:T(8,128)(2,1)}, u32[]{:S(2)}) copy-start(bf16[1024,128]{1,0:T(8,128)(2,1)} %constant.20.clone.back_ref) | copy-start | bytes 786436
  0.7 28.3 %copy-start.1 = (bf16[1,64,64,128]{3,2,1,0:T(8,128)(2,1)S(1)}, bf16[1,64,64,128]{3,2,1,0:T(8,128)(2,1)}, u32[]{:S(2)}) copy-start(bf16[1,64,64,128]{3,2,1,0:T(8,128)(2,1)} %param.17) | copy-start | bytes 3145732
  0.7 47.3 %copy-start.3 = (bf16[512,64]{1,0:T(8,128)(2,1)S(1)}, bf16[512,64]{1,0:T(8,128)(2,1)}, u32[]{:S(2)}) copy-start(bf16[512,64]{1,0:T(8,128)(2,1)} %constant.23.clone.spread_ref) | copy-start | bytes 196612
  0.7 47.3 %copy-start.9 = (bf16[128,512]{1,0:T(8,128)(2,1)S(1)}, bf16[128,512]{1,0:T(8,128)(2,1)}, u32[]{:S(2)}) copy-start(bf16[128,512]{1,0:T(8,128)(2,1)} %constant.21.clone.synth_ref) | copy-start | bytes 393220
  0.7 47.3 %copy-start.10 = (bf16[512,128]{1,0:T(8,128)(2,1)S(1)}, bf16[512,128]{1,0:T(8,128)(2,1)}, u32[]{:S(2)}) copy-start(bf16[512,128]{1,0:T(8,128)(2,1)} %constant.22.clone.table_ref) | copy-start | bytes 393220
  0.7 47.3 %copy-start.11 = (bf16[64,64]{1,0:T(8,128)(2,1)S(1)}, bf16[64,64]{1,0:T(8,128)(2,1)}, u32[]{:S(2)}) copy-start(bf16[64,64]{1,0:T(8,128)(2,1)} %weight_ref.3) | copy-start | bytes 24580
  4.0 43.9 %copy-start = (bf16[4,64,8,512]{3,2,1,0:T(8,128)(2,1)S(1)}, bf16[4,64,8,512]{3,2,1,0:T(8,128)(2,1)}, u32[]{:S(2)}) copy-start(bf16[4,64,8,512]{3,2,1,0:T(8,128)(2,1)} %param.15) | copy-start | bytes 6291460
  4.1 43.9 %copy-start.2 = (bf16[4,64,8,512]{3,2,1,0:T(8,128)(2,1)S(1)}, bf16[4,64,8,512]{3,2,1,0:T(8,128)(2,1)}, u32[]{:S(2)}) copy-start(bf16[4,64,8,512]{3,2,1,0:T(8,128)(2,1)} %param.16) | copy-start | bytes 6291460
  4.1 43.9 %copy-start.12 = (f32[64]{0:T(128)S(1)}, f32[64]{0:T(128)}, u32[]{:S(2)}) copy-start(f32[64]{0:T(128)} %param.19) | copy-start | bytes 772
  48.0 22.8 %copy-start.4 = (bf16[128,1024]{1,0:T(8,128)(2,1)S(1)}, bf16[128,1024]{1,0:T(8,128)(2,1)}, u32[]{:S(2)}) copy-start(bf16[128,1024]{1,0:T(8,128)(2,1)} %constant.24.clone.into_ref) | copy-start | bytes 786436
  48.0 22.8 %copy-start.5 = (bf16[1024,128]{1,0:T(8,128)(2,1)S(1)}, bf16[1024,128]{1,0:T(8,128)(2,1)}, u32[]{:S(2)}) copy-start(bf16[1024,128]{1,0:T(8,128)(2,1)} %constant.25.clone.back_ref) | copy-start | bytes 786436
  72.8 18.3 %all-to-all-start.3 = ((bf16[128,16,128]{2,1,0:T(8,128)(2,1)}), bf16[128,16,128]{2,1,0:T(8,128)(2,1)S(1)}, u32[]{:S(2)}, u32[]{:S(2)}) async-start(bf16[128,16,128]{2,1,0:T(8,128)(2,1)} %bitcast.30), calls=%async_computation.3 | async-start | bytes 1048576 | tf_op jit(solution)/shard_map/all_to_all | solution.py:397
  79.1 12.0 %copy-start.8 = (bf16[128,512]{1,0:T(8,128)(2,1)S(1)}, bf16[128,512]{1,0:T(8,128)(2,1)}, u32[]{:S(2)}) copy-start(bf16[128,512]{1,0:T(8,128)(2,1)} %constant.26.clone.synth_ref) | copy-start | bytes 393220
where the time goes:
time: 93.3 us; the launch traced here: 93.1 us
  blocking collectives  60.2 us (65%)
  Pallas kernels  17.4 us (19%)
  waiting for transfers between devices  9.9 us (11%)
  starting transfers between devices  4.61 us (5%)
    all_to_all x3, blocking collectives, exchange(): lax.all_to_all(tiles, AXES, split_axis=0, concat_axis=0, tiled=True)  60.2 us
    all_to_all x1, waiting for transfers between devices, exchange(): lax.all_to_all(tiles, AXES, split_axis=0, concat_axis=0, tiled=True)  9.9 us
    pallas_call x1, Pallas kernels, slab_stage(): pl.pallas_call(functools.partial(slab_kernel, slab, planes, 16), out_shap...  5.09 us
    all_to_all x1, starting transfers between devices, exchange(): lax.all_to_all(tiles, AXES, split_axis=0, concat_axis=0, tiled=True)  4.61 us
    pallas_call x2, Pallas kernels, owner(): pl.pallas_call(functools.partial(owner_kernel, forward, slab), out_shape=...  3.34 us
    pallas_call x1, Pallas kernels, analysis(): pl.pallas_call(functools.partial(analysis_kernel, slab, pieces), out_shap...  3.32 us
    pallas_call x1, Pallas kernels, weight_grad(): pl.pallas_call(functools.partial(weight_grad_kernel, step_channels), out_...  2.07 us
    pallas_call x1, Pallas kernels, final_stage(): pl.pallas_call(functools.partial(final_kernel, slab, planes), out_shape=p...  1.96 us
  transfers between devices with their start and end apart: 1, of which 1 were waited for; matrix products, arithmetic and copies ran while one was open for 0% of the time, Pallas kernels for 4%

commit v1 on v0

--- a/solution.py
+++ b/solution.py
@@ -117,7 +117,13 @@
     return jnp.where(row == col, full, 0.0).astype(jnp.bfloat16)
 
 
-def owner_kernel(forward, slab, blocks_ref, into_ref, back_ref, weight_ref, out_ref, modes_ref, kept, mixed, partial, out, sems):
+def owner_kernel(forward, slab, blocks_ref, into_ref, back_ref, weight_ref, *refs):
+    if forward:
+        out_ref, modes_ref, kept, mixed, partial, out, sems = refs
+    else:
+        waiting_ref, out_ref, modes_ref, stored_ref, kept, mixed, partial, out, sems = refs
+        store = pltpu.make_async_copy(waiting_ref, stored_ref, sems.at[4])
+        store.start()
     peers = blocks_ref.shape[0] // (2 * slab)
     channels = weight_ref.shape[0]
     planes = 2 * LANES // channels
@@ -171,9 +177,12 @@
             sent[i].start()
     for copy in sent:
         copy.wait()
-
-
-def owner(blocks, into, back, weight, forward):
+    if not forward:
+        store.wait()
+
+
+def owner(blocks, into, back, weight, *waiting):
+    forward = not waiting
     cells, modes = back.shape
     rows = blocks.shape[0]
     channels = weight.shape[0]
@@ -183,30 +192,27 @@
         out_shape=(
             (jax.ShapeDtypeStruct if forward else pltpu.MemorySpace.HBM)(blocks.shape, jnp.bfloat16),
             jax.ShapeDtypeStruct((2 * LANES, modes), jnp.bfloat16),
-        ),
-        in_specs=[EVERY] * 4,
-        out_specs=(EVERY if forward else ANYWHERE, EVERY),
+        )
+        + tuple(pltpu.MemorySpace.HBM(array.shape, array.dtype) for array in waiting),
+        in_specs=[EVERY] * (4 + len(waiting)),
+        out_specs=(EVERY if forward else ANYWHERE, EVERY) + (ANYWHERE,) * len(waiting),
         scratch_shapes=[
             pltpu.VMEM((2 * LANES, modes), jnp.float32),
             pltpu.VMEM((2 * LANES, modes), jnp.float32),
             pltpu.VMEM((8 if forward else 8 * 2 * LANES, modes), jnp.float32),
             pltpu.VMEM((16, LANES) if forward else blocks.shape, jnp.bfloat16),
-            pltpu.SemaphoreType.DMA((4,)),
+            pltpu.SemaphoreType.DMA((5,)),
         ],
         compiler_params=params(),
         cost_estimate=pl.CostEstimate(flops=4 * rows * LANES * modes, bytes_accessed=4 << 20, transcendentals=0),
         name="owner_forward" if forward else "owner_backward",
-    )(blocks, into, back, weight)
+    )(blocks, into, back, weight, *waiting)
 
 
 def slab_kernel(slab, planes, chunk, blocks_ref, field_ref, weight_ref, spread_ref, bias_ref, cotangent_ref, synth_ref,
-                table_ref, out_hbm, grad_ref, send_ref, by_peer, by_rows, half_rows, pre_even, pre_odd, matrix, offset, out,
-                out_sems):
+                table_ref, out, grad_ref, send_ref, by_peer, by_rows, half_rows, pre_even, pre_odd, matrix, offset):
     plane_rows = out.shape[0] // planes
     rows = plane_rows // 2
-
-    def out_copy(i):
-        return pltpu.make_async_copy(part_of(out, i, 2 * planes), part_of(out_hbm, i, 2 * planes), out_sems.at[i])
 
     def fill(target, z, half):
         start = z * plane_rows + half * rows
@@ -225,7 +231,6 @@
             out[there, :] = (value * share).astype(out.dtype)
             slope = share + value * bell * DENSITY
             grad_ref[there, :] = (cotangent_ref[there, :].astype(jnp.float32) * slope).astype(grad_ref.dtype)
-        out_copy(2 * z + half).start()
 
     def analyse(z, half):
         here = pl.ds(z * plane_rows + half * rows, rows)
@@ -250,8 +255,6 @@
     for half in range(2):
         rows_to_blocks(half, slab, half_rows, by_peer)
     send_ref[...] = by_peer[...].astype(send_ref.dtype)
-    for i in range(2 * planes):
-        out_copy(i).wait()
 
 
 def spread_table(channels, slab):
@@ -269,12 +272,12 @@
     return pl.pallas_call(
         functools.partial(slab_kernel, slab, planes, 16),
         out_shape=(
-            pltpu.MemorySpace.HBM(whole, jnp.bfloat16),
+            jax.ShapeDtypeStruct(whole, jnp.bfloat16),
             jax.ShapeDtypeStruct(whole, jnp.bfloat16),
             jax.ShapeDtypeStruct(blocks.shape, jnp.bfloat16),
         ),
         in_specs=[EVERY] * 8,
-        out_specs=(ANYWHERE, EVERY, EVERY),
+        out_specs=(EVERY, EVERY, EVERY),
         scratch_shapes=[
             pltpu.VMEM((total, modes), jnp.float32),
             pltpu.VMEM((total, modes), jnp.float32),
@@ -283,8 +286,6 @@
             pltpu.VMEM((rows // 2, cells), jnp.float32),
             pltpu.VMEM((rows, rows), jnp.bfloat16),
             pltpu.VMEM((rows, 1), jnp.float32),
-            pltpu.VMEM(whole, jnp.bfloat16),
-            pltpu.SemaphoreType.DMA((2 * planes,)),
         ],
         compiler_params=params(),
         cost_estimate=pl.CostEstimate(flops=4 * total * cells * modes, bytes_accessed=11 << 20, transcendentals=2 * total * cells),
@@ -416,13 +417,13 @@
     bias = channel_bias[None, :]
 
     received = exchange(analysis(field, jnp.asarray(forward_y)), devices)
-    modal, coeffs = owner(received, flip(forward_x), jnp.asarray(inverse_x), weight, True)
+    modal, coeffs = owner(received, flip(forward_x), jnp.asarray(inverse_x), weight)
     gathered = exchange(modal, devices)
     output, grad_pre, grad_rows = slab_stage(
         gathered, field, gradient, local_weight, bias, flip(inverse_y), jnp.asarray(inverse_y)
     )
     received = exchange(grad_rows, devices)
-    partial, grads = owner(received, flip(inverse_x), jnp.asarray(forward_x), weight, False)
+    partial, grads, output = owner(received, flip(inverse_x), jnp.asarray(forward_x), weight, output)
     gathered = exchange(partial, devices)
     grad_weight = weight_grad(coeffs.astype(jnp.float32), grads.astype(jnp.float32), channels)
     grad_field = final_stage(gathered, pointwise(grad_pre, local_weight), flip(forward_y))

time: 93.3 us -> 92.9 us (level)
  no operation moved by 1% of the time
where the time goes in v1:
time: 92.9 us; the launch traced here: 92.7 us
  blocking collectives  60.2 us (65%)
  Pallas kernels  17 us (18%)
  waiting for transfers between devices  9.9 us (11%)
  starting transfers between devices  4.61 us (5%)
    all_to_all x3, blocking collectives, exchange(): lax.all_to_all(tiles, AXES, split_axis=0, concat_axis=0, tiled=True)  60.2 us
    all_to_all x1, waiting for transfers between devices, exchange(): lax.all_to_all(tiles, AXES, split_axis=0, concat_axis=0, tiled=True)  9.9 us
    pallas_call x1, Pallas kernels, slab_stage(): pl.pallas_call(functools.partial(slab_kernel, slab, planes, 16), out_shap...  4.67 us
    all_to_all x1, starting transfers between devices, exchange(): lax.all_to_all(tiles, AXES, split_axis=0, concat_axis=0, tiled=True)  4.61 us
    pallas_call x2, Pallas kernels, owner(): pl.pallas_call(functools.partial(owner_kernel, forward, slab), out_shape=...  3.36 us
    pallas_call x1, Pallas kernels, analysis(): pl.pallas_call(functools.partial(analysis_kernel, slab, pieces), out_shap...  3.32 us
    pallas_call x1, Pallas kernels, weight_grad(): pl.pallas_call(functools.partial(weight_grad_kernel, step_channels), out_...  2.07 us
    pallas_call x1, Pallas kernels, final_stage(): pl.pallas_call(functools.partial(final_kernel, slab, planes), out_shape=p...  1.96 us
  transfers between devices with their start and end apart: 1, of which 1 were waited for; matrix products, arithmetic and copies ran while one was open for 0% of the time, Pallas kernels for 4%

profile of v1, /device:TPU:1, one launch (start us, length us, event | category | flops | bytes accessed | tf_op | source)
XLA Modules:
  0.0 92.7 jit_solution(9267989937239373958)
XLA Ops:
  0.6 0.0 copy-start.6
  0.6 0.0 copy-start.7
  0.7 0.0 copy-start.3
  0.7 0.0 copy-start.9
  0.7 0.0 copy-start.10
  0.7 3.3 %analysis.1 = bf16[2048,128]{1,0:T(8,128)(2,1)S(1)} custom-call(bf16[2048,512]{1,0:T(8,128)(2,1)} %bitcast.15, bf16[512,128]{1,0:T(8,128)(2,1)} %constant.18.clone.table_hbm), custom_call_target="tpu_custom_call" | custom-call | flops 268435456 | bytes 3145728 | tf_op jit(solution)/shard_map/analysis/pallas_call | solution.py:93
  4.0 0.0 copy-start
  4.1 0.0 copy-start.2
  4.1 0.0 copy-start.12
  4.1 24.9 %all_to_all.20 = bf16[128,16,128]{2,1,0:T(8,128)(2,1)S(1)} all-to-all(bf16[128,16,128]{2,1,0:T(8,128)(2,1)S(1)} %bitcast.21), channel_id=1, replica_groups=mesh['gx'=16,'gy'=8] {'gx','gy'}, dimensions={0} | all-to-all | bytes 1048576 | tf_op jit(solution)/shard_map/all_to_all | solution.py:398
  28.9 0.0 copy-done.1
  29.0 1.4 %owner_forward.1 = (bf16[2048,128]{1,0:T(8,128)(2,1)S(1)}, bf16[256,128]{1,0:T(8,128)(2,1)S(1)}) custom-call(bf16[2048,128]{1,0:T(8,128)(2,1)S(1)} %bitcast.20, bf16[128,1024]{1,0:T(8,128)(2,1)S(1)} %copy-done.6, bf16[1024,128]{1,0:T(8,128)(2,1)S(1)} %copy-done.7, bf16[64,64,128]{2,1,0:T(8,128)(2,1)S(1)} %bitcast.17), custom_call_target="tpu_custom_call" | custom-call | flops 134217728 | bytes 4194304 | tf_op jit(solution)/shard_map/owner_forward/pallas_call | solution.py:190
  30.3 17.7 %all_to_all.21 = bf16[128,16,128]{2,1,0:T(8,128)(2,1)S(1)} all-to-all(bf16[128,16,128]{2,1,0:T(8,128)(2,1)S(1)} %bitcast.26), channel_id=1, replica_groups=mesh['gx'=16,'gy'=8] {'gx','gy'}, dimensions={0} | all-to-all | bytes 1048576 | tf_op jit(solution)/shard_map/all_to_all | solution.py:398
  48.0 0.0 copy-start.4
  48.0 0.0 copy-start.5
  48.0 4.7 %slab_stage.1 = (bf16[2048,512]{1,0:T(8,128)(2,1)S(1)}, bf16[2048,512]{1,0:T(8,128)(2,1)S(1)}, bf16[2048,128]{1,0:T(8,128)(2,1)S(1)}) custom-call(bf16[2048,128]{1,0:T(8,128)(2,1)S(1)} %bitcast.24, bf16[2048,512]{1,0:T(8,128)(2,1)S(1)} %bitcast.16, bf16[64,64]{1,0:T(8,128)(2,1)S(1)} %copy-done.11, bf16[512,64]{1,0:T(8,128)(2,1)S(1)} %copy-done.3, ...), custom_call_target="tpu_custom_call" | custom-call | flops 536870912 | bytes 11534336 | tf_op jit(solution)/shard_map/slab_stage/pallas_call | solution.py:272
  52.7 17.7 %all_to_all.22 = bf16[128,16,128]{2,1,0:T(8,128)(2,1)S(1)} all-to-all(bf16[128,16,128]{2,1,0:T(8,128)(2,1)S(1)} %bitcast.25), channel_id=1, replica_groups=mesh['gx'=16,'gy'=8] {'gx','gy'}, dimensions={0} | all-to-all | bytes 1048576 | tf_op jit(solution)/shard_map/all_to_all | solution.py:398
  70.4 2.0 %owner_backward.1 = (bf16[2048,128]{1,0:T(8,128)(2,1)}, bf16[256,128]{1,0:T(8,128)(2,1)S(1)}, bf16[2048,512]{1,0:T(8,128)(2,1)}) custom-call(bf16[2048,128]{1,0:T(8,128)(2,1)S(1)} %bitcast.23, bf16[128,1024]{1,0:T(8,128)(2,1)S(1)} %copy-done.4, bf16[1024,128]{1,0:T(8,128)(2,1)S(1)} %copy-done.5, bf16[64,64,128]{2,1,0:T(8,128)(2,1)S(1)} %bitcast.18, ...), custom_call_target="tpu_custom_call" | custom-call | flops 134217728 | bytes 4194304 | tf_op jit(solution)/shard_map/owner_backward/pallas_call | solution.py:190
  72.4 4.6 %all-to-all-start.3 = ((bf16[128,16,128]{2,1,0:T(8,128)(2,1)}), bf16[128,16,128]{2,1,0:T(8,128)(2,1)S(1)}, u32[]{:S(2)}, u32[]{:S(2)}) async-start(bf16[128,16,128]{2,1,0:T(8,128)(2,1)} %bitcast.30), calls=%async_computation.3 | async-start | bytes 1048576 | tf_op jit(solution)/shard_map/all_to_all | solution.py:398
  77.0 1.7 %pointwise.1.through_ref = bf16[2048,512]{1,0:T(8,128)(2,1)S(1)} custom-call(bf16[2048,512]{1,0:T(8,128)(2,1)S(1)} %get-tuple-element.16.field_ref, bf16[64,64]{1,0:T(8,128)(2,1)S(1)} %copy-done.11, bf16[512,64]{1,0:T(8,128)(2,1)S(1)} %copy-done.3), custom_call_target="tpu_custom_call", output_to_operand_aliasing={{}: (0, {})} | custom-call | flops 1073741824 | bytes 6291456 | tf_op jit(solution)/shard_map/pointwise/pallas_call | solution.py:312
  78.7 0.0 copy-start.8
  78.7 2.1 %weight_grad.1 = f32[64,64,128]{2,1,0:T(8,128)} custom-call(f32[256,128]{1,0:T(8,128)S(1)} %convert_element_type.6.coeffs_ref, f32[256,128]{1,0:T(8,128)S(1)} %convert_element_type.7.grads_ref), custom_call_target="tpu_custom_call" | custom-call | flops 4194304 | bytes 5242880 | tf_op jit(solution)/shard_map/weight_grad/pallas_call | solution.py:384
  80.8 9.9 %all-to-all-done.3 = bf16[128,16,128]{2,1,0:T(8,128)(2,1)S(1)} async-done(((bf16[128,16,128]{2,1,0:T(8,128)(2,1)}), bf16[128,16,128]{2,1,0:T(8,128)(2,1)S(1)}, u32[]{:S(2)}, u32[]{:S(2)}) %all-to-all-start.3) | async-done | bytes 524320 | tf_op jit(solution)/shard_map/all_to_all | solution.py:398
  90.7 2.0 %final_stage.1 = bf16[2048,512]{1,0:T(8,128)(2,1)} custom-call(bf16[2048,128]{1,0:T(8,128)(2,1)S(1)} %bitcast.19, bf16[2048,512]{1,0:T(8,128)(2,1)S(1)} %pointwise.1.through_ref, bf16[128,512]{1,0:T(8,128)(2,1)S(1)} %copy-done.8), custom_call_target="tpu_custom_call" | custom-call | flops 268435456 | bytes 7340032 | tf_op jit(solution)/shard_map/final_stage/pallas_call | solution.py:346
  (16 shorter events, 0.1 us)
Async XLA Ops:
  0.6 28.3 %copy-start.6 = (bf16[128,1024]{1,0:T(8,128)(2,1)S(1)}, bf16[128,1024]{1,0:T(8,128)(2,1)}, u32[]{:S(2)}) copy-start(bf16[128,1024]{1,0:T(8,128)(2,1)} %constant.19.clone.into_ref) | copy-start | bytes 786436
  0.6 28.3 %copy-start.7 = (bf16[1024,128]{1,0:T(8,128)(2,1)S(1)}, bf16[1024,128]{1,0:T(8,128)(2,1)}, u32[]{:S(2)}) copy-start(bf16[1024,128]{1,0:T(8,128)(2,1)} %constant.20.clone.back_ref) | copy-start | bytes 786436
  0.7 28.3 %copy-start.1 = (bf16[1,64,64,128]{3,2,1,0:T(8,128)(2,1)S(1)}, bf16[1,64,64,128]{3,2,1,0:T(8,128)(2,1)}, u32[]{:S(2)}) copy-start(bf16[1,64,64,128]{3,2,1,0:T(8,128)(2,1)} %param.17) | copy-start | bytes 3145732
  0.7 47.3 %copy-start.3 = (bf16[512,64]{1,0:T(8,128)(2,1)S(1)}, bf16[512,64]{1,0:T(8,128)(2,1)}, u32[]{:S(2)}) copy-start(bf16[512,64]{1,0:T(8,128)(2,1)} %constant.23.clone.spread_ref) | copy-start | bytes 196612
  0.7 47.3 %copy-start.9 = (bf16[128,512]{1,0:T(8,128)(2,1)S(1)}, bf16[128,512]{1,0:T(8,128)(2,1)}, u32[]{:S(2)}) copy-start(bf16[128,512]{1,0:T(8,128)(2,1)} %constant.21.clone.synth_ref) | copy-start | bytes 393220
  0.7 47.3 %copy-start.10 = (bf16[512,128]{1,0:T(8,128)(2,1)S(1)}, bf16[512,128]{1,0:T(8,128)(2,1)}, u32[]{:S(2)}) copy-start(bf16[512,128]{1,0:T(8,128)(2,1)} %constant.22.clone.table_ref) | copy-start | bytes 393220
  0.7 47.3 %copy-start.11 = (bf16[64,64]{1,0:T(8,128)(2,1)S(1)}, bf16[64,64]{1,0:T(8,128)(2,1)}, u32[]{:S(2)}) copy-start(bf16[64,64]{1,0:T(8,128)(2,1)} %weight_ref.3) | copy-start | bytes 24580
  4.0 43.9 %copy-start = (bf16[4,64,8,512]{3,2,1,0:T(8,128)(2,1)S(1)}, bf16[4,64,8,512]{3,2,1,0:T(8,128)(2,1)}, u32[]{:S(2)}) copy-start(bf16[4,64,8,512]{3,2,1,0:T(8,128)(2,1)} %param.15) | copy-start | bytes 6291460
  4.1 43.9 %copy-start.2 = (bf16[4,64,8,512]{3,2,1,0:T(8,128)(2,1)S(1)}, bf16[4,64,8,512]{3,2,1,0:T(8,128)(2,1)}, u32[]{:S(2)}) copy-start(bf16[4,64,8,512]{3,2,1,0:T(8,128)(2,1)} %param.16) | copy-start | bytes 6291460
  4.1 43.9 %copy-start.12 = (f32[64]{0:T(128)S(1)}, f32[64]{0:T(128)}, u32[]{:S(2)}) copy-start(f32[64]{0:T(128)} %param.19) | copy-start | bytes 772
  48.0 22.4 %copy-start.4 = (bf16[128,1024]{1,0:T(8,128)(2,1)S(1)}, bf16[128,1024]{1,0:T(8,128)(2,1)}, u32[]{:S(2)}) copy-start(bf16[128,1024]{1,0:T(8,128)(2,1)} %constant.24.clone.into_ref) | copy-start | bytes 786436
  48.0 22.3 %copy-start.5 = (bf16[1024,128]{1,0:T(8,128)(2,1)S(1)}, bf16[1024,128]{1,0:T(8,128)(2,1)}, u32[]{:S(2)}) copy-start(bf16[1024,128]{1,0:T(8,128)(2,1)} %constant.25.clone.back_ref) | copy-start | bytes 786436
  72.4 18.3 %all-to-all-start.3 = ((bf16[128,16,128]{2,1,0:T(8,128)(2,1)}), bf16[128,16,128]{2,1,0:T(8,128)(2,1)S(1)}, u32[]{:S(2)}, u32[]{:S(2)}) async-start(bf16[128,16,128]{2,1,0:T(8,128)(2,1)} %bitcast.30), calls=%async_computation.3 | async-start | bytes 1048576 | tf_op jit(solution)/shard_map/all_to_all | solution.py:398
  78.7 12.0 %copy-start.8 = (bf16[128,512]{1,0:T(8,128)(2,1)S(1)}, bf16[128,512]{1,0:T(8,128)(2,1)}, u32[]{:S(2)}) copy-start(bf16[128,512]{1,0:T(8,128)(2,1)} %constant.26.clone.synth_ref) | copy-start | bytes 393220
